TPU v7x, 32 devices: a whole 2x2x4 slice. The times are simulated.
32 devices in a mesh: rep: 4 (over y, x), fsdp: 8 (over z, core).
Axes of the slice: x: 2, y: 2, z: 4, core: 2. Of those that a mesh axis runs over, the one named last changes fastest.
Arguments:
- states: bfloat16 [128, 32, 5120], P('fsdp'), may hold values from -6 to 6
- labels: bfloat16 [128, 8], P('fsdp'), may hold values from -4 to 4
- lengths: int32 [128], P('fsdp'), may hold values from 1 to 32
- segments: int32 [128, 32], P('fsdp'), may hold values from 0 to 7, never falling along the last dimension, each value on 1 to 8 neighbouring positions
- destinations: int32 [128, 1], P('fsdp'), may hold values from 0 to 7; in each aligned block of 16 rows (0 to 15, 16 to 31, ...) at most 2 rows name the same one
- gain: float32 [5120], replicated, may hold values from 0.1 to 1.9
- head_in: bfloat16 [5120, 5120], P('fsdp', 'rep'), may hold values from -0.078125 to 0.078125
- head_out: float32 [5120], P('rep'), may hold values from -0.078125 to 0.078125
Outputs:
- step_rewards: float32 [128, 8], P('fsdp')
- head_grad: float32 [5120, 5120], P('fsdp', 'rep')
Inputs may be any that keep to these rules, and one draw needn't show every extreme that they name: `destinations`: among the 16 rows of one generator device no trainer index is named by more than 2 rows, a bound that some block reaches. `segments`: step numbers never fall along a row; every step has 1 to 8 slots, one step of each row exactly 8.
All inputs are finite; a program needn't handle non-finite values.
Results may differ from a plain program's by a relative error of at most 0.0052.
Values may be sent and summed in bfloat16 or wider, within the bound.
No kernel may reach another device: no remote copies, remote signals or barrier semaphores. Data moves between devices by JAX's collectives and lax.ppermute only.
A program may use at most 128 MiB of HBM per device.

v0:
```python
import math

import jax
import jax.numpy as jnp
from jax import lax
from jax.sharding import PartitionSpec as P

CAP = 2
STEPS = 8


def silu_slope(pre_act):
    sigma = jax.nn.sigmoid(pre_act)
    return sigma * (1.0 + pre_act * (1.0 - sigma))


def normalize(tokens_flat, gain):
    wide = tokens_flat.astype(jnp.float32)
    meansq = jnp.mean(wide * wide, axis=1, keepdims=True)
    return (wide * lax.rsqrt(meansq + 1e-06) * gain[None, :]).astype(jnp.bfloat16)


def local(states, labels, lengths, segments, destinations, gain, head_in, head_out):
    row_count, slot_span, feature_width = states.shape
    trainers = lax.axis_size("fsdp")
    slot_total = trainers * CAP
    target = destinations[:, 0]
    order = jnp.arange(row_count, dtype=jnp.int32)
    earlier = (target[:, None] == target[None, :]) & (order[None, :] < order[:, None])
    rank_in = jnp.sum(earlier.astype(jnp.int32), axis=1)
    placing = (target * CAP + rank_in)[None, :] == jnp.arange(slot_total, dtype=jnp.int32)[:, None]
    place_int = placing.astype(jnp.int32)
    place_half = placing.astype(jnp.bfloat16)
    seg_sent = jnp.dot(place_int, segments).reshape(trainers, CAP, slot_span)
    len_sent = jnp.dot(place_int, lengths).reshape(trainers, CAP)
    label_sent = jnp.dot(place_half, labels, preferred_element_type=jnp.float32).astype(
        jnp.bfloat16
    )
    label_sent = label_sent.reshape(trainers, CAP, STEPS)
    seg_got, len_got = (
        lax.all_to_all(seg_sent, "fsdp", split_axis=0, concat_axis=0, tiled=True),
        lax.all_to_all(len_sent, "fsdp", split_axis=0, concat_axis=0, tiled=True),
    )
    packed = jnp.dot(place_half, states.reshape(row_count, -1), preferred_element_type=jnp.float32)
    packed = packed.astype(jnp.bfloat16).reshape(trainers, CAP, slot_span, feature_width)
    arrived, label_got = (
        lax.all_to_all(packed, "fsdp", split_axis=0, concat_axis=0, tiled=True),
        lax.all_to_all(label_sent, "fsdp", split_axis=0, concat_axis=0, tiled=True),
    )
    normed = normalize(arrived.reshape(-1, feature_width), gain)
    seg_rows = seg_got.reshape(slot_total, slot_span)
    len_rows = len_got.reshape(slot_total)
    positions = jnp.arange(slot_span, dtype=jnp.int32)
    valid = (positions[None, :] < len_rows[:, None]).astype(jnp.float32)
    step_ids = jnp.arange(STEPS, dtype=jnp.int32)
    member = (seg_rows[:, :, None] == step_ids[None, None, :]).astype(jnp.float32) * valid[
        :, :, None
    ]
    live = jnp.max(member, axis=1)

    def add_rows(weight_piece):
        return jnp.dot(normed, weight_piece, preferred_element_type=jnp.float32)

    pre_act = add_rows(lax.all_gather(head_in, "fsdp", axis=0, tiled=True))
    partial_score = jnp.sum(jax.nn.silu(pre_act) * head_out[None, :], axis=1)
    score = lax.psum(partial_score, "rep").reshape(slot_total, slot_span)
    step_score = jnp.einsum("rs,rsk->rk", score, member, precision=lax.Precision.HIGHEST)
    step_error = live * (step_score - label_got.reshape(slot_total, STEPS).astype(jnp.float32))
    token_error = jnp.einsum(
        "rk,rsk->rs", step_error, member, precision=lax.Precision.HIGHEST
    ).reshape(-1)
    pre_grad = (token_error[:, None] * head_out[None, :] * silu_slope(pre_act)).astype(jnp.bfloat16)
    rate = 0.5 / math.sqrt(row_count * trainers * slot_span)
    head_grad = lax.psum_scatter(
        lax.dot_general(
            normed, pre_grad, (((0,), (0,)), ((), ())), preferred_element_type=jnp.float32
        ),
        "fsdp",
        scatter_dimension=0,
        tiled=True,
    )
    fresh = (head_in.astype(jnp.float32) - rate * head_grad).astype(jnp.bfloat16)
    pre_fresh = add_rows(lax.all_gather(fresh, "fsdp", axis=0, tiled=True))
    partial_fresh = jnp.sum(jax.nn.silu(pre_fresh) * head_out[None, :], axis=1)
    fresh_score = lax.psum(partial_fresh, "rep").reshape(slot_total, slot_span)
    step_rewards = jnp.einsum("rs,rsk->rk", fresh_score, member, precision=lax.Precision.HIGHEST)
    return (step_rewards, head_grad)


def solution(mesh):
    in_specs = (
        P("fsdp", None, None),
        P("fsdp", None),
        P("fsdp"),
        P("fsdp", None),
        P("fsdp", None),
        P(),
        P("fsdp", "rep"),
        P("rep"),
    )
    out_specs = (P("fsdp", None), P("fsdp", "rep"))
    return jax.shard_map(local, mesh=mesh, in_specs=in_specs, out_specs=out_specs, check_vma=False)
```

profile of v0, /device:TPU:0, one launch (start us, length us, event | category | flops | bytes accessed | tf_op | source)
XLA Modules:
  0.0 708.1 jit_solution(2607554561009971989)
XLA Ops:
  7.2 0.7 all-gather.3.cloned.1.call-update
  7.9 0.9 convert_reduce_fusion
  9.5 0.8 convolution_bitcast_fusion
  10.3 0.7 all_to_all.17
  11.0 6.3 all-to-all-start.2
  17.3 0.7 fusion.22
  18.0 8.2 %copy.22 = bf16[2,8,32,5120]{3,1,2,0:T(8,128)(2,1)} copy(bf16[2,8,32,5120]{3,2,1,0:T(8,128)(2,1)} %bitcast.52) | data formatting | bytes 10485760
  26.2 5.1 all-to-all-start.1
  31.4 4.0 convolution_convert_fusion
  35.3 5.2 copy.23
  40.5 5.4 all-to-all-start
  46.1 0.7 copy.15
  48.2 195.8 %all-to-all-done = bf16[8,2,32,5120]{3,2,1,0:T(8,128)(2,1)} async-done(((bf16[8,2,32,5120]{3,2,1,0:T(8,128)(2,1)}), bf16[8,2,32,5120]{3,2,1,0:T(8,128)(2,1)}, u32[]{:S(2)}, u32[]{:S(2)}) %all-to-all-start) | async-done | bytes 5242912 | tf_op jit(solution)/shard_map/all_to_all | solution.py:47
  244.0 3.3 all-to-all-start.3
  247.5 3.6 multiply_reduce_fusion
  251.2 6.8 fusion.1
  258.1 13.9 %multiply_reduce_fusion.2 = (f32[512]{0:T(512)S(1)}, f32[512,1280]{1,0:T(8,128)}) fusion(f32[1280]{0:T(1024)S(1)} %copy-done.5, bf16[512,5120]{1,0:T(8,128)(2,1)} %fusion.1, bf16[5120,1280]{1,0:T(8,128)(2,1)} %all-gather.3.cloned.1.call-done), kind=kOutput, calls=%fused_computation.8 | convolution fusion | flops 6714818048 | bytes 20978688 | tf_op jit(solution)/shard_map/dot_general | solution.py:62
  272.0 10.0 %psum.14 = f32[16,32]{1,0:T(8,128)S(1)} all-reduce(f32[16,32]{1,0:T(8,128)S(1)} %reshape.91), channel_id=1, replica_groups=mesh['rep'=4,'fsdp'=8] {'rep'}, use_global_device_ids=true, to_apply=%region_4.5 | all-reduce | flops 512 | bytes 4096 | tf_op jit(solution)/shard_map/psum | solution.py:66
  282.6 15.3 %fusion.2 = f32[5120,1280]{1,0:T(8,128)} fusion(bf16[512,5120]{1,0:T(8,128)(2,1)} %fusion.1, f32[512,1280]{1,0:T(8,128)} %get-tuple-element.3, f32[512]{0:T(512)S(1)} %mul.99, f32[1280]{0:T(1024)S(1)} %copy-done.5), kind=kOutput, calls=%fused_computation.10 | convolution fusion | flops 6717440000 | bytes 34085888 | tf_op jit(solution)/shard_map/dot_general | solution.py:75
  298.2 256.2 %reduce-scatter.2.cloned.1.call-done = f32[640,1280]{1,0:T(8,128)} async-done(((f32[5120,1280]{1,0:T(8,128)}), f32[640,1280]{1,0:T(8,128)}) %reduce-scatter.2.cloned.1.call-update) | async-done | bytes 3276816 | tf_op jit(solution)/shard_map/reduce_scatter | solution.py:74
  554.4 3.6 subtract_convert_fusion
  558.1 119.5 %all-gather.5.cloned.1.call-done = bf16[5120,1280]{1,0:T(8,128)(2,1)} async-done(((bf16[640,1280]{1,0:T(8,128)(2,1)}), bf16[5120,1280]{1,0:T(8,128)(2,1)}) %all-gather.5.cloned.1.call-update) | async-done | bytes 13107216 | tf_op jit(solution)/shard_map/all_gather | solution.py:83
  677.6 12.9 %multiply_reduce_fusion.1 = f32[512]{0:T(512)S(1)} fusion(f32[1280]{0:T(1024)S(1)} %copy-done.5, bf16[512,5120]{1,0:T(8,128)(2,1)} %fusion.1, bf16[5120,1280]{1,0:T(8,128)(2,1)} %all-gather.5.cloned.1.call-done), kind=kOutput, calls=%fused_computation.6 | convolution fusion | flops 6714818048 | bytes 18357248 | tf_op jit(solution)/shard_map/dot_general | solution.py:62
  690.6 10.0 %psum.15 = f32[16,32]{1,0:T(8,128)S(1)} all-reduce(f32[16,32]{1,0:T(8,128)S(1)} %reshape.93), channel_id=1, replica_groups=mesh['rep'=4,'fsdp'=8] {'rep'}, use_global_device_ids=true, to_apply=%region_7.8 | all-reduce | flops 512 | bytes 4096 | tf_op jit(solution)/shard_map/psum | solution.py:85
  (38 shorter events, 4.6 us)
Async XLA Ops:
  7.2 10.1 %copy-start = (s32[16,32]{1,0:T(8,128)S(1)}, s32[16,32]{1,0:T(8,128)}, u32[]{:S(2)}) copy-start(s32[16,32]{1,0:T(8,128)} %param.11) | copy-start | bytes 6148
  7.2 250.9 %all-gather.3.cloned.1.call-start = ((), (), s32[]{:S(2)}) async-start(), calls=%async_computation.5 | async-start | bytes 14745600 | tf_op jit(solution)/shard_map/all_gather | solution.py:64
  11.0 15.3 %all-to-all-start.2 = ((s32[8,1,2]{2,1,0:T(1,128)}), s32[8,1,2]{2,1,0:T(1,128)S(1)}, u32[]{:S(2)}, u32[]{:S(2)}) async-start(s32[8,1,2]{2,1,0:T(1,128)} %bitcast.6), calls=%async_computation.2 | async-start | bytes 8192 | tf_op jit(solution)/shard_map/all_to_all | solution.py:42
  26.2 14.3 %all-to-all-start.1 = ((s32[8,2,32]{2,1,0:T(2,128)}), s32[8,2,32]{2,1,0:T(2,128)S(1)}, u32[]{:S(2)}, u32[]{:S(2)}) async-start(s32[8,2,32]{2,1,0:T(2,128)} %bitcast.2), calls=%async_computation.1 | async-start | bytes 16384 | tf_op jit(solution)/shard_map/all_to_all | solution.py:41
  40.5 5.4 copy-start.4
  40.5 203.4 %all-to-all-start = ((bf16[8,2,32,5120]{3,2,1,0:T(8,128)(2,1)}), bf16[8,2,32,5120]{3,2,1,0:T(8,128)(2,1)}, u32[]{:S(2)}, u32[]{:S(2)}) async-start(bf16[8,2,32,5120]{3,2,1,0:T(8,128)(2,1)} %bitcast.51), calls=%async_computation | async-start | bytes 10485760 | tf_op jit(solution)/shard_map/all_to_all | solution.py:47
  46.0 205.3 %copy-start.3 = (f32[5120]{0:T(1024)S(1)}, f32[5120]{0:T(1024)}, u32[]{:S(2)}) copy-start(f32[5120]{0:T(1024)} %param.13) | copy-start | bytes 61444
  244.0 38.3 %all-to-all-start.3 = ((bf16[8,2,8]{2,1,0:T(2,128)(2,1)}), bf16[8,2,8]{2,1,0:T(2,128)(2,1)S(1)}, u32[]{:S(2)}, u32[]{:S(2)}) async-start(bf16[8,2,8]{2,1,0:T(2,128)(2,1)} %bitcast.11), calls=%async_computation.3 | async-start | bytes 8192 | tf_op jit(solution)/shard_map/all_to_all | solution.py:48
  247.3 307.1 %reduce-scatter.2.cloned.1.call-start = ((), (), s32[]{:S(2)}) async-start(), calls=%async_computation.6 | async-start | bytes 29491200 | tf_op jit(solution)/shard_map/reduce_scatter | solution.py:74
  251.2 6.9 copy-start.5
  297.9 256.5 %copy-start.2 = (bf16[640,1280]{1,0:T(8,128)(2,1)S(1)}, bf16[640,1280]{1,0:T(8,128)(2,1)}, u32[]{:S(2)}) copy-start(bf16[640,1280]{1,0:T(8,128)(2,1)} %param.14) | copy-start | bytes 4915204
  297.9 379.7 %all-gather.5.cloned.1.call-start = ((), (), s32[]{:S(2)}) async-start(), calls=%async_computation.7 | async-start | bytes 14745600 | tf_op jit(solution)/shard_map/all_gather | solution.py:83
  677.6 23.9 %copy-start.1 = (s32[16,32]{1,0:T(8,128)S(1)}, s32[16,32]{1,0:T(8,128)}, u32[]{:S(2)}) copy-start(s32[16,32]{1,0:T(8,128)} %param.11) | copy-start | bytes 6148
Sparse Core Ops, SparseCore 0:
  9.7 221.4 all-gather.2
  298.1 256.3 reduce-scatter.1
  558.2 119.3 all-gather.4
where the time goes:
time: 709 us; the launch traced here: 708 us
  waiting for transfers between devices  572 us (81%)
  matrix products  48.5 us (7%)
  starting transfers between devices  20.7 us (3%)
  blocking collectives  19.9 us (3%)
  other arithmetic  16.5 us (2%)
  local copies, waits for them, and re-layouts  16.4 us (2%)
  between operations  13.9 us (2%)
    reduce_scatter x1, waiting for transfers between devices, local(): lax.psum_scatter(lax.dot_general(normed, pre_grad, (((0,), (0,)), ((), ()...  256 us
    all_to_all x1, waiting for transfers between devices, local(): lax.all_to_all(packed, 'fsdp', split_axis=0, concat_axis=0, tiled=True)  196 us
    all_gather x1, waiting for transfers between devices, local(): pre_fresh = add_rows(lax.all_gather(fresh, 'fsdp', axis=0, tiled=True))  120 us
    dot_general x2, matrix products, add_rows(): return jnp.dot(normed, weight_piece, preferred_element_type=jnp.float32)  26.8 us
    dot_general x1, matrix products, local(): lax.dot_general(normed, pre_grad, (((0,), (0,)), ((), ())), preferred_ele...  15.3 us
  transfers between devices with their start and end apart: 7, of which 3 were waited for; matrix products, arithmetic and copies ran while one was open for 7% of the time, Pallas kernels for 0%

commit v1 on v0

v1 whole, which is shorter than its diff:
```python
import math

import jax
import jax.numpy as jnp
from jax import lax
from jax.sharding import PartitionSpec as P

CAP = 2
STEPS = 8
CHUNKS = 2


def silu_slope(pre_act):
    sigma = jax.nn.sigmoid(pre_act)
    return sigma * (1.0 + pre_act * (1.0 - sigma))


def normalize(tokens_flat, gain):
    wide = tokens_flat.astype(jnp.float32)
    meansq = jnp.mean(wide * wide, axis=1, keepdims=True)
    return (wide * lax.rsqrt(meansq + 1e-06) * gain[None, :]).astype(jnp.bfloat16)


def member_of(segments, lengths):
    positions = jnp.arange(segments.shape[1], dtype=jnp.int32)
    valid = (positions[None, :] < lengths[:, None]).astype(jnp.float32)
    step_ids = jnp.arange(STEPS, dtype=jnp.int32)
    return (segments[:, :, None] == step_ids[None, None, :]).astype(jnp.float32) * valid[:, :, None]


def rank_of(target):
    order = jnp.arange(target.shape[0], dtype=jnp.int32)
    earlier = (target[:, None] == target[None, :]) & (order[None, :] < order[:, None])
    return jnp.sum(earlier.astype(jnp.int32), axis=1)


def gathered_weights(states, labels, lengths, segments, destinations, gain, head_in, head_out):
    row_count, slot_span, feature_width = states.shape
    trainers = lax.axis_size("fsdp")
    slot_total = trainers * CAP
    normed = normalize(states.reshape(-1, feature_width), gain)
    member = member_of(segments, lengths)
    live = jnp.max(member, axis=1)

    def scored(weights):
        pre_act = jnp.dot(normed, weights, preferred_element_type=jnp.float32)
        partial = jnp.sum(jax.nn.silu(pre_act) * head_out[None, :], axis=1)
        return pre_act, lax.psum(partial, "rep").reshape(row_count, slot_span)

    pre_act, score = scored(lax.all_gather(head_in, "fsdp", axis=0, tiled=True))
    step_score = jnp.einsum("rs,rsk->rk", score, member, precision=lax.Precision.HIGHEST)
    step_error = live * (step_score - labels.astype(jnp.float32))
    token_error = jnp.einsum("rk,rsk->rs", step_error, member, precision=lax.Precision.HIGHEST).reshape(-1)
    pre_grad = (token_error[:, None] * head_out[None, :] * silu_slope(pre_act)).astype(jnp.bfloat16)
    rate = 0.5 / math.sqrt(row_count * trainers * slot_span)
    head_grad = lax.psum_scatter(
        lax.dot_general(normed, pre_grad, (((0,), (0,)), ((), ())), preferred_element_type=jnp.float32),
        "fsdp",
        scatter_dimension=0,
        tiled=True,
    )
    fresh = (head_in.astype(jnp.float32) - rate * head_grad).astype(jnp.bfloat16)
    _, fresh_score = scored(lax.all_gather(fresh, "fsdp", axis=0, tiled=True))
    reward = jnp.einsum("rs,rsk->rk", fresh_score, member, precision=lax.Precision.HIGHEST)
    target = destinations[:, 0]
    slot = target * CAP + rank_of(target)
    placing = (slot[None, :] == jnp.arange(slot_total, dtype=jnp.int32)[:, None]).astype(jnp.float32)
    placed = jnp.dot(placing, reward, precision=lax.Precision.HIGHEST)
    return lax.all_to_all(placed, "fsdp", split_axis=0, concat_axis=0, tiled=True), head_grad


X_MATE = [(r, r ^ 1) for r in range(4)]
Y_MATE = [(r, r ^ 2) for r in range(4)]
XY_MATE = [(r, r ^ 3) for r in range(4)]
CORE_MATE = [(f, f ^ 1) for f in range(8)]
Z1_MATE = [(f, f ^ 2) for f in range(8)]
Z2_MATE = [(f, f ^ 4) for f in range(8)]
Z3_MATE = [(f, f ^ 6) for f in range(8)]
INNER = [(f, f ^ 6) for f in (2, 3, 4, 5)]
OUTWARD = [(f, f ^ 2) for f in (2, 3, 4, 5)]


def sum_everywhere(values):
    values = values + lax.ppermute(values, "fsdp", CORE_MATE)
    values = (values + lax.ppermute(values, "rep", X_MATE)) + (
        lax.ppermute(values, "rep", Y_MATE) + lax.ppermute(values, "rep", XY_MATE)
    )
    return (values + lax.ppermute(values, "fsdp", Z1_MATE)) + (
        lax.ppermute(values, "fsdp", Z2_MATE) + lax.ppermute(values, "fsdp", Z3_MATE)
    )


def gather_small(values):
    f = lax.axis_index("fsdp")
    mates = [values] + [
        lax.ppermute(values, "fsdp", [(i, i ^ j) for i in range(8)]) for j in range(1, 8)
    ]
    stacked = jnp.stack(mates)
    order = jnp.arange(8, dtype=jnp.int32) ^ f
    return jnp.sum(
        jnp.where((order[:, None] == jnp.arange(8)[None, :])[:, :, None], stacked[None], 0.0), axis=1
    )


def spread_tokens(local, states, labels, lengths, segments, destinations, gain, head_in, head_out):
    row_count, slot_span, width = states.shape
    f = lax.axis_index("fsdp")
    r = lax.axis_index("rep")
    z = f // 2
    c = f % 2
    inner = (z == 1) | (z == 2)
    hidden = head_in.shape[1] // 8
    depth = head_in.shape[0]

    counts = jnp.sum(member_of(segments, lengths), axis=1)
    target = destinations[:, 0]
    slot_of = target * (8 * CAP) + f * CAP + rank_of(target)
    facts = jnp.concatenate(
        [counts.reshape(-1), labels.astype(jnp.float32).reshape(-1), slot_of.astype(jnp.float32)]
    )
    facts = jnp.pad(facts, (0, 384 - facts.shape[0]))
    facts_all = gather_small(facts)
    steps = row_count * STEPS
    counts_all = facts_all[:, :steps]
    labels_all = facts_all[:, steps : 2 * steps]
    slots_all = facts_all[:, 2 * steps : 2 * steps + row_count].reshape(-1)
    live_all = jnp.minimum(counts_all, 1.0)
    upto = jnp.arange(steps)[:, None] >= jnp.arange(steps)[None, :]
    ends_all = jnp.sum(jnp.where(upto[None], counts_all[:, None, :], 0.0), axis=2)

    ends_row = jnp.sum(
        jnp.where(
            jnp.arange(row_count)[:, None] >= jnp.arange(row_count)[None, :], lengths[None, :], 0
        ),
        axis=1,
    )
    place = jnp.where(
        jnp.arange(slot_span)[None, :] < lengths[:, None],
        (ends_row - lengths)[:, None] + jnp.arange(slot_span)[None, :],
        -1,
    ).reshape(-1)
    picks = (place[None, :] == jnp.arange(local, dtype=jnp.int32)[:, None]).astype(jnp.bfloat16)
    tokens = jnp.dot(picks, states.reshape(-1, width), preferred_element_type=jnp.float32)
    own = normalize(tokens.astype(jnp.bfloat16), gain)

    head_pieces = jnp.transpose(head_in).reshape(8, hidden, depth)
    head_got = lax.all_to_all(head_pieces, "fsdp", split_axis=0, concat_axis=0, tiled=True)
    head_t = jnp.transpose(head_got.reshape(8, hidden, depth), (1, 0, 2)).reshape(hidden, width)
    out_share = lax.dynamic_slice_in_dim(head_out, f * hidden, hidden)[:, None]

    quarter = local // 4
    piece = quarter // CHUNKS
    half = piece // 16 * 8
    mine = lax.dynamic_slice_in_dim(own, r * quarter, quarter)
    groups = [[own, lax.ppermute(own, "fsdp", CORE_MATE)]]
    arrived = {"a": [], "b": [], "c": []}

    def in_plane(part):
        from_x = lax.ppermute(part, "rep", X_MATE)
        from_y = lax.ppermute(part, "rep", Y_MATE)
        diag_low = lax.ppermute(from_x[:half], "rep", Y_MATE)
        diag_high = lax.ppermute(from_y[half:], "rep", X_MATE)
        return jnp.concatenate([part, from_x, from_y, diag_low, diag_high])

    for chunk in range(CHUNKS):
        part = mine[chunk * piece : (chunk + 1) * piece]
        first = lax.ppermute(part, "fsdp", Z1_MATE)
        first_in = lax.ppermute(part, "fsdp", INNER)
        second_out = lax.ppermute(first_in, "fsdp", OUTWARD)
        second_in = lax.ppermute(first, "fsdp", INNER)
        third_out = lax.ppermute(second_in, "fsdp", OUTWARD)
        for name, got in (
            ("a", first),
            ("b", jnp.where(inner, first_in, second_out)),
            ("c", jnp.where(inner, second_in, third_out)),
        ):
            full = in_plane(got)
            arrived[name].append(full)
            arrived[name].append(lax.ppermute(full, "fsdp", CORE_MATE))
    for name in "abc":
        groups.append(arrived[name])
    groups = [jnp.concatenate(parts) for parts in groups]

    lower = z < 2
    sources = [z, z ^ 1, jnp.where(lower, 2, 1), jnp.where(lower, 3, 0)]
    place_own = jnp.arange(local, dtype=jnp.int32)
    in_piece = jnp.arange(piece, dtype=jnp.int32)
    place_chunks = [
        jnp.concatenate([(r ^ j) * quarter + chunk * piece + in_piece for j in range(4)])
        for chunk in range(CHUNKS)
    ]

    def step_bounds(source, core):
        take = jnp.arange(8) == source * 2 + core
        ends = jnp.sum(jnp.where(take[:, None], ends_all, 0.0), axis=0)
        counts_here = jnp.sum(jnp.where(take[:, None], counts_all, 0.0), axis=0)
        return ends - counts_here, ends

    marks = []
    for index in range(4):
        cores = []
        for core in (c, 1 - c):
            low, high = step_bounds(sources[index], core)
            cores.append((low, high))
        rows = []
        if index == 0:
            rows = [(place_own, 0), (place_own, 1)]
        else:
            for chunk in range(CHUNKS):
                rows += [(place_chunks[chunk], 0), (place_chunks[chunk], 1)]
        masks = [
            (spot[None, :].astype(jnp.float32) >= cores[which][0][:, None])
            & (spot[None, :].astype(jnp.float32) < cores[which][1][:, None])
            for spot, which in rows
        ]
        marks.append((rows, masks))

    def onto_steps(scores):
        total = jnp.zeros((8, steps), jnp.float32)
        for index in range(4):
            rows, masks = marks[index]
            sums = [jnp.zeros((steps,), jnp.float32)] * 2
            at = 0
            for (spot, which), mask in zip(rows, masks):
                span = spot.shape[0]
                piece_score = scores[index][at : at + span]
                sums[which] = sums[which] + jnp.sum(jnp.where(mask, piece_score[None, :], 0.0), axis=1)
                at += span
            for which, core in ((0, c), (1, 1 - c)):
                take = jnp.arange(8) == sources[index] * 2 + core
                total = total + jnp.where(take[:, None], sums[which][None, :], 0.0)
        return total

    def onto_tokens(values):
        spread = []
        for index in range(4):
            rows, masks = marks[index]
            here = []
            for core in (c, 1 - c):
                take = jnp.arange(8) == sources[index] * 2 + core
                here.append(jnp.sum(jnp.where(take[:, None], values, 0.0), axis=0))
            spread.append(
                jnp.concatenate(
                    [
                        jnp.sum(jnp.where(mask, here[which][:, None], 0.0), axis=0)
                        for (spot, which), mask in zip(rows, masks)
                    ]
                )
            )
        return spread

    def forward(weights_t):
        return [
            lax.dot_general(
                weights_t, group, (((1,), (1,)), ((), ())), preferred_element_type=jnp.float32
            )
            for group in groups
        ]

    pres = forward(head_t)
    part_scores = [jnp.sum(jax.nn.silu(pre) * out_share, axis=0) for pre in pres]
    step_score = sum_everywhere(onto_steps(part_scores))
    step_error = live_all * (step_score - labels_all)
    errors = onto_tokens(step_error)
    grad_t = jnp.zeros((hidden, width), jnp.float32)
    for pre, error, group in zip(pres, errors, groups):
        pre_grad = (error[None, :] * out_share * silu_slope(pre)).astype(jnp.bfloat16)
        grad_t = grad_t + jnp.dot(pre_grad, group, preferred_element_type=jnp.float32)
    rate = 0.5 / math.sqrt(row_count * 8 * slot_span)
    fresh_t = (head_t.astype(jnp.float32) - rate * grad_t).astype(jnp.bfloat16)

    grad_pieces = jnp.transpose(grad_t.astype(jnp.bfloat16).reshape(hidden, 8, depth), (1, 0, 2))
    grad_got = lax.all_to_all(grad_pieces, "fsdp", split_axis=0, concat_axis=0, tiled=True)
    head_grad = jnp.transpose(grad_got.reshape(8 * hidden, depth)).astype(jnp.float32)

    fresh_scores = [jnp.sum(jax.nn.silu(pre) * out_share, axis=0) for pre in forward(fresh_t)]
    reward = sum_everywhere(onto_steps(fresh_scores)).reshape(8 * row_count, STEPS)
    wanted = f * (8 * CAP) + jnp.arange(8 * CAP, dtype=jnp.int32)
    hits = slots_all[None, :] == wanted[:, None].astype(jnp.float32)
    step_rewards = jnp.sum(jnp.where(hits[:, :, None], reward[None], 0.0), axis=1)
    return step_rewards, head_grad


def solution(mesh):
    in_specs = (
        P("fsdp", None, None),
        P("fsdp", None),
        P("fsdp"),
        P("fsdp", None),
        P("fsdp", None),
        P(),
        P("fsdp", "rep"),
        P("rep"),
    )
    out_specs = (P("fsdp", None), P("fsdp", "rep"))

    def local(states, *rest):
        if lax.axis_size("rep") == 4 and lax.axis_size("fsdp") == 8:
            return spread_tokens(states.shape[0] * states.shape[1], states, *rest)
        return gathered_weights(states, *rest)

    return jax.shard_map(local, mesh=mesh, in_specs=in_specs, out_specs=out_specs, check_vma=False)
```

time: 709 us -> 424 us (0.60)
  waiting for transfers between devices: 572 us -> 180 us
  starting transfers between devices: 20.7 us -> 69.6 us
  local copies, waits for them, and re-layouts: 16.4 us -> 59.8 us
  matrix products: 48.5 us -> 87.9 us
  blocking collectives: 19.9 us -> 0 us
  between operations: 13.9 us -> 2.03 us
    reduce_scatter x1 -> x0, waiting for transfers between devices: 256 us -> none  [local(): lax.psum_scatter(lax.dot_general(normed, pre_grad, (((0,), (0,)), ((), ()...]
    all_to_all x4 -> x2, waiting for transfers between devices: 196 us -> 0.01 us  [the longest x1 0.01 us: spread_tokens(): lax.all_to_all(head_pieces, 'fsdp', split_axis=0, concat_axis=0, tiled=True)]
    ppermute x0 -> x62, waiting for transfers between devices: none -> 180 us  [the longest x6 48.3 us: in_plane(): diag_low = lax.ppermute(from_x[:half], 'rep', Y_MATE)]
    all_gather x2 -> x0, waiting for transfers between devices: 120 us -> none  [the longest x1 120 us: local(): pre_fresh = add_rows(lax.all_gather(fresh, 'fsdp', axis=0, tiled=True))]
    ppermute x0 -> x62, starting transfers between devices: none -> 61.7 us  [the longest x2 7.77 us: spread_tokens(): first = lax.ppermute(part, 'fsdp', Z1_MATE)]
    dot_general x10 -> x13, matrix products: 48.5 us -> 87.9 us  [the longest x8 56.1 us: forward(): lax.dot_general(weights_t, group, (((1,), (1,)), ((), ())), preferred_ele...]
    unnamed x14 -> x96, local copies, waits for them, and re-layouts: 13.5 us -> 39.3 us
    psum x2 -> x0, blocking collectives: 19.9 us -> none  [the longest x1 9.97 us: local(): fresh_score = lax.psum(partial_fresh, 'rep').reshape(slot_total, slot_span)]
  transfers between devices with their start and end apart: 7 -> 64, of which waited for: 3 -> 24; matrix products, arithmetic and copies ran while one was open for 7% -> 22% of each run, Pallas kernels for 0% -> 0%
where the time goes in v1:
time: 424 us; the launch traced here: 417 us
  waiting for transfers between devices  180 us (42%)
  matrix products  87.9 us (21%)
  starting transfers between devices  69.6 us (16%)
  local copies, waits for them, and re-layouts  59.8 us (14%)
  other arithmetic  18.2 us (4%)
    dot_general x8, matrix products, forward(): lax.dot_general(weights_t, group, (((1,), (1,)), ((), ())), preferred_ele...  56.1 us
    ppermute x6, waiting for transfers between devices, in_plane(): diag_low = lax.ppermute(from_x[:half], 'rep', Y_MATE)  48.3 us
    ppermute x7, waiting for transfers between devices, gather_small(): lax.ppermute(values, 'fsdp', [(i, i ^ j) for i in range(8)])  46.1 us
    unnamed x96, local copies, waits for them, and re-layouts  39.3 us
    ppermute x2, waiting for transfers between devices, spread_tokens(): second_out = lax.ppermute(first_in, 'fsdp', OUTWARD)  25.8 us
    dot_general x4, matrix products, spread_tokens(): jnp.dot(pre_grad, group, preferred_element_type=jnp.float32)  24.6 us
    ppermute x2, waiting for transfers between devices, spread_tokens(): third_out = lax.ppermute(second_in, 'fsdp', OUTWARD)  22.5 us
    ppermute x6, waiting for transfers between devices, in_plane(): diag_high = lax.ppermute(from_y[half:], 'rep', X_MATE)  13.3 us
  transfers between devices with their start and end apart: 64, of which 24 were waited for; matrix products, arithmetic and copies ran while one was open for 22% of the time, Pallas kernels for 0%

profile of v1, /device:TPU:0, one launch (start us, length us, event | category | flops | bytes accessed | tf_op | source)
XLA Modules:
  0.0 417.3 jit_solution(14083068470644096652)
XLA Ops:
  2.9 7.2 %fusion = (f32[512]{0:T(512)S(1)}, bf16[512,5120]{1,0:T(8,128)(2,1)}) fusion(bf16[512,5120]{1,0:T(8,128)(2,1)} %bitcast.57, s32[512]{0:T(512)S(1)} %select_n.331), kind=kOutput, calls=%fused_computation.2 | convolution fusion | flops 2695101952 | bytes 10489856 | tf_op jit(solution)/shard_map/dot_general | solution.py:143
  10.2 6.8 %fusion.2 = bf16[512,5120]{1,0:T(8,128)(2,1)} fusion(bf16[512,5120]{1,0:T(8,128)(2,1)} %get-tuple-element.200, f32[5120]{0:T(1024)S(1)} %copy-done.24, f32[512]{0:T(512)S(1)} %add_rsqrt_fusion), kind=kLoop, calls=%fused_computation.4 | loop fusion | flops 10485760 | bytes 10508288 | tf_op jit(solution)/shard_map/convert_element_type | solution.py:21
  20.2 5.9 %collective-permute-start.8 = (bf16[64,5120]{1,0:T(8,128)(2,1)}, bf16[64,5120]{1,0:T(8,128)(2,1)}, u32[]{:S(2)}, u32[]{:S(2)}) collective-permute-start(bf16[64,5120]{1,0:T(8,128)(2,1)} %get-tuple-element.116), channel_id=1, source_target_pairs={{0,2},{1,3},{2,0},{3,1},{4,6},{5,7},{6,4},{7,5},{8,10},{9,11},{10,... | collective-permute-start | bytes 1966088 | tf_op jit(solution)/shard_map/ppermute | solution.py:167
  36.7 6.5 %collective-permute-done.1 = f32[384]{0:T(512)S(1)} collective-permute-done((f32[384]{0:T(512)S(1)}, f32[384]{0:T(512)S(1)}, u32[]{:S(2)}, u32[]{:S(2)}) %collective-permute-start.1) | collective-permute-done | bytes 1568 | tf_op jit(solution)/shard_map/ppermute | solution.py:96
  43.9 36.8 %collective-permute-done.3 = f32[384]{0:T(512)S(1)} collective-permute-done((f32[384]{0:T(512)S(1)}, f32[384]{0:T(512)S(1)}, u32[]{:S(2)}, u32[]{:S(2)}) %collective-permute-start.3) | collective-permute-done | bytes 1568 | tf_op jit(solution)/shard_map/ppermute | solution.py:96
  96.0 10.1 %collective-permute-done.21 = bf16[64,5120]{1,0:T(8,128)(2,1)S(1)} collective-permute-done((bf16[64,5120]{1,0:T(8,128)(2,1)S(1)}, bf16[64,5120]{1,0:T(8,128)(2,1)S(1)}, u32[]{:S(2)}, u32[]{:S(2)}) %collective-permute-start.21) | collective-permute-done | bytes 655392 | tf_op jit(solution)/shard_map/ppermute | solution.py:169
  107.5 15.8 %collective-permute-done.28 = bf16[64,5120]{1,0:T(8,128)(2,1)S(1)} collective-permute-done((bf16[64,5120]{1,0:T(8,128)(2,1)}, bf16[64,5120]{1,0:T(8,128)(2,1)S(1)}, u32[]{:S(2)}, u32[]{:S(2)}) %collective-permute-start.28) | collective-permute-done | bytes 655392 | tf_op jit(solution)/shard_map/ppermute | solution.py:169
  134.1 16.7 %collective-permute-done.11 = bf16[32,5120]{1,0:T(8,128)(2,1)S(1)} collective-permute-done((bf16[32,5120]{1,0:T(8,128)(2,1)S(1)}, bf16[32,5120]{1,0:T(8,128)(2,1)S(1)}, u32[]{:S(2)}, u32[]{:S(2)}) %collective-permute-start.11) | collective-permute-done | bytes 327712 | tf_op jit(solution)/shard_map/ppermute | solution.py:161
  156.0 11.7 %collective-permute-done.35 = bf16[64,5120]{1,0:T(8,128)(2,1)S(1)} collective-permute-done((bf16[64,5120]{1,0:T(8,128)(2,1)S(1)}, bf16[64,5120]{1,0:T(8,128)(2,1)S(1)}, u32[]{:S(2)}, u32[]{:S(2)}) %collective-permute-start.35) | collective-permute-done | bytes 655392 | tf_op jit(solution)/shard_map/ppermute | solution.py:171
  170.7 10.8 %collective-permute-done.42 = bf16[64,5120]{1,0:T(8,128)(2,1)S(1)} collective-permute-done((bf16[64,5120]{1,0:T(8,128)(2,1)S(1)}, bf16[64,5120]{1,0:T(8,128)(2,1)S(1)}, u32[]{:S(2)}, u32[]{:S(2)}) %collective-permute-start.42) | collective-permute-done | bytes 655392 | tf_op jit(solution)/shard_map/ppermute | solution.py:171
  191.0 22.6 %collective-permute-done.24 = bf16[32,5120]{1,0:T(8,128)(2,1)S(1)} collective-permute-done((bf16[32,5120]{1,0:T(8,128)(2,1)S(1)}, bf16[32,5120]{1,0:T(8,128)(2,1)S(1)}, u32[]{:S(2)}, u32[]{:S(2)}) %collective-permute-start.24) | collective-permute-done | bytes 327712 | tf_op jit(solution)/shard_map/ppermute | solution.py:161
  230.7 9.1 %collective-permute-done.38 = bf16[32,5120]{1,0:T(8,128)(2,1)} collective-permute-done((bf16[32,5120]{1,0:T(8,128)(2,1)}, bf16[32,5120]{1,0:T(8,128)(2,1)}, u32[]{:S(2)}, u32[]{:S(2)}) %collective-permute-start.38) | collective-permute-done | bytes 327712 | tf_op jit(solution)/shard_map/ppermute | solution.py:161
  242.1 6.3 %collective-permute-done.39 = bf16[32,5120]{1,0:T(8,128)(2,1)S(1)} collective-permute-done((bf16[32,5120]{1,0:T(8,128)(2,1)}, bf16[32,5120]{1,0:T(8,128)(2,1)S(1)}, u32[]{:S(2)}, u32[]{:S(2)}) %collective-permute-start.39) | collective-permute-done | bytes 327712 | tf_op jit(solution)/shard_map/ppermute | solution.py:162
  283.0 7.7 %convolution_bitcast_fusion.1 = f32[160,1024]{1,0:T(8,128)S(1)} fusion(bf16[1024,5120]{1,0:T(8,128)(2,1)} %constant_dynamic-update-slice_fusion.32, bf16[160,5120]{1,0:T(8,128)(2,1)S(1)} %bitcast.49), kind=kOutput, calls=%fused_computation.17 | convolution fusion | flops 1677721600 | bytes 12779520 | tf_op jit(solution)/shard_map/dot_general | solution.py:254
  292.4 8.0 %convolution_bitcast_fusion = f32[160,1024]{1,0:T(8,128)S(1)} fusion(bf16[1024,5120]{1,0:T(8,128)(2,1)} %constant_dynamic-update-slice_fusion.54, bf16[160,5120]{1,0:T(8,128)(2,1)S(1)} %bitcast.50), kind=kOutput, calls=%fused_computation.16 | convolution fusion | flops 1677721600 | bytes 12779520 | tf_op jit(solution)/shard_map/dot_general | solution.py:254
  300.5 7.3 %multiply_reduce_fusion.7 = (f32[1024]{0:T(1024)S(1)}, f32[1024]{0:T(1024)S(1)}, f32[1024]{0:T(1024)S(1)}, f32[1024]{0:T(1024)S(1)}, f32[160,1024]{1,0:T(8,128)S(1)}) fusion(f32[160]{0:T(256)S(1)} %dynamic_slice.6, f32[160,1024]{1,0:T(8,128)S(1)} %convolution_bitcast_fusion.2, f32[160,1024]{1,0:T(8,128)S(1)} %convolution_bitcast_fusion.1, ...), kind=kOutput, calls=%fused_computation.34 | convolution fusion | flops 1702621184 | bytes 14762624 | tf_op jit(solution)/shard_map/dot_general | solution.py:254
  329.9 6.1 %fusion.10 = f32[160,5120]{1,0:T(8,128)S(1)} fusion(bf16[1024,5120]{1,0:T(8,128)(2,1)} %constant_dynamic-update-slice_fusion.32, f32[160,1024]{1,0:T(8,128)S(1)} %convolution_bitcast_fusion.1, f32[1024]{0:T(1024)S(1)} %pad_maximum_fusion.10, f32[160]{0:T(256)S(1)} %dynamic_slice.6), kind=kOutput, calls=%fused_computation.43 | convolution fusion | flops 1679360000 | bytes 14422656 | tf_op jit(solution)/shard_map/dot_general | solution.py:268
  336.1 7.9 %fusion.11 = f32[160,5120]{1,0:T(8,128)} fusion(bf16[1024,5120]{1,0:T(8,128)(2,1)} %constant_dynamic-update-slice_fusion.54, f32[160,1024]{1,0:T(8,128)S(1)} %convolution_bitcast_fusion, f32[1024]{0:T(1024)S(1)} %pad_maximum_fusion.11, f32[160]{0:T(256)S(1)} %dynamic_slice.6), kind=kOutput, calls=%fused_computation.44 | convolution fusion | flops 1679360000 | bytes 14422656 | tf_op jit(solution)/shard_map/dot_general | solution.py:268
  344.3 6.8 %fusion.34 = (bf16[160,5120]{1,0:T(8,128)(2,1)S(1)}, bf16[160,5120]{1,0:T(8,128)(2,1)S(1)}) fusion(bf16[160,5120]{1,0:T(8,128)(2,1)S(1)} %bitcast.52, f32[160,5120]{1,0:T(8,128)} %fusion.11, f32[160,5120]{1,0:T(8,128)S(1)} %fusion.10, f32[160,5120]{1,0:T(8,128)S(1)} %copy-done.29, bf16[512,5120]{1,0:T(8,128)(2,1)} %collective-permute-done.7, ...), kind=kOutput, calls=%fused_computation.264 | convolution fusion | flops 1706885120 | bytes 25891456 | tf_op jit(solution)/shard_map/dot_general | solution.py:268
  351.1 7.6 %fusion.44 = f32[160,1024]{1,0:T(8,128)S(1)} fusion(bf16[160,5120]{1,0:T(8,128)(2,1)S(1)} %get-tuple-element.118, bf16[1024,5120]{1,0:T(8,128)(2,1)} %constant_dynamic-update-slice_fusion.54), kind=kOutput, calls=%fused_computation.274 | convolution fusion | flops 1677721600 | bytes 12779520 | tf_op jit(solution)/shard_map/dot_general | solution.py:254
  358.6 7.6 %fusion.43 = f32[160,1024]{1,0:T(8,128)S(1)} fusion(bf16[160,5120]{1,0:T(8,128)(2,1)S(1)} %get-tuple-element.118, bf16[1024,5120]{1,0:T(8,128)(2,1)} %constant_dynamic-update-slice_fusion.32), kind=kOutput, calls=%fused_computation.273 | convolution fusion | flops 1677721600 | bytes 12779520 | tf_op jit(solution)/shard_map/dot_general | solution.py:254
  371.8 7.9 %multiply_reduce_fusion.2 = (f32[1024]{0:T(1024)S(1)}, f32[1024]{0:T(1024)S(1)}, f32[1024]{0:T(1024)S(1)}) fusion(f32[160]{0:T(256)S(1)} %dynamic_slice.6, f32[160,1024]{1,0:T(8,128)S(1)} %fusion.43, f32[160,1024]{1,0:T(8,128)S(1)} %fusion.44, bf16[160,5120]{1,0:T(8,128)(2,1)S(1)} %get-tuple-element.118, bf16[1024,5120]{1,0:T(8,128)(2,1)} %copy-done.23), kind=kOutput, calls=%fused_computation.22 | convolution fusion | flops 1680667648 | bytes 13447808 | tf_op jit(solution)/shard_map/dot_general | solution.py:254
  380.4 6.5 %multiply_reduce_fusion.3 = f32[1024]{0:T(1024)S(1)} fusion(bf16[160,5120]{1,0:T(8,128)(2,1)S(1)} %get-tuple-element.118, bf16[512,5120]{1,0:T(8,128)(2,1)} %collective-permute-done.7, bf16[512,5120]{1,0:T(8,128)(2,1)} %fusion.2, f32[160]{0:T(256)S(1)} %dynamic_slice.6), kind=kOutput, calls=%fused_computation.23 | convolution fusion | flops 1699675136 | bytes 12128896 | tf_op jit(solution)/shard_map/dot_general | solution.py:254
  399.4 11.9 %collective-permute-done.60 = f32[8,128]{1,0:T(8,128)S(1)} collective-permute-done((f32[8,128]{1,0:T(8,128)S(1)}, f32[8,128]{1,0:T(8,128)S(1)}, u32[]{:S(2)}, u32[]{:S(2)}) %collective-permute-start.60) | collective-permute-done | bytes 4128 | tf_op jit(solution)/shard_map/ppermute | solution.py:89
  (341 shorter events, 164.0 us)
Async XLA Ops:
  19.5 68.5 %collective-permute-start.20 = (bf16[64,5120]{1,0:T(8,128)(2,1)}, bf16[64,5120]{1,0:T(8,128)(2,1)S(1)}, u32[]{:S(2)}, u32[]{:S(2)}) collective-permute-start(bf16[64,5120]{1,0:T(8,128)(2,1)} %get-tuple-element.116), channel_id=1, source_target_pairs={{2,4},{3,5},{4,2},{5,3},{10,12},{11,13},{12,10},{13,11},{18,20},{1... | collective-permute-start | bytes 1966088 | tf_op jit(solution)/shard_map/ppermute | solution.py:168
  20.2 69.4 %collective-permute-start.8 = (bf16[64,5120]{1,0:T(8,128)(2,1)}, bf16[64,5120]{1,0:T(8,128)(2,1)}, u32[]{:S(2)}, u32[]{:S(2)}) collective-permute-start(bf16[64,5120]{1,0:T(8,128)(2,1)} %get-tuple-element.116), channel_id=1, source_target_pairs={{0,2},{1,3},{2,0},{3,1},{4,6},{5,7},{6,4},{7,5},{8,10},{9,11},{10,... | collective-permute-start | bytes 1966088 | tf_op jit(solution)/shard_map/ppermute | solution.py:167
  30.9 199.5 %all-to-all-start = ((bf16[8,160,640]{2,1,0:T(8,128)(2,1)}), bf16[8,160,640]{2,1,0:T(8,128)(2,1)S(1)}, u32[]{:S(2)}, u32[]{:S(2)}) async-start(bf16[8,160,640]{2,1,0:T(8,128)(2,1)} %bitcast.2), calls=%async_computation | async-start | bytes 3276800 | tf_op jit(solution)/shard_map/all_to_all | solution.py:147
  34.8 57.8 %collective-permute-start.14 = (bf16[64,5120]{1,0:T(8,128)(2,1)}, bf16[64,5120]{1,0:T(8,128)(2,1)S(1)}, u32[]{:S(2)}, u32[]{:S(2)}) collective-permute-start(bf16[64,5120]{1,0:T(8,128)(2,1)} %get-tuple-element.115), channel_id=1, source_target_pairs={{0,2},{1,3},{2,0},{3,1},{4,6},{5,7},{6,4},{7,5},{8,10},{9,11},{10,... | collective-permute-start | bytes 1966088 | tf_op jit(solution)/shard_map/ppermute | solution.py:167
  43.2 37.6 %collective-permute-start.3 = (f32[384]{0:T(512)S(1)}, f32[384]{0:T(512)S(1)}, u32[]{:S(2)}, u32[]{:S(2)}) collective-permute-start(f32[384]{0:T(512)S(1)} %select_maximum_fusion), channel_id=1, source_target_pairs={{0,4},{1,5},{2,6},{3,7},{4,0},{5,1},{6,2},{7,3},{8,12},{9,13},{10,... | collective-permute-start | bytes 4616 | tf_op jit(solution)/shard_map/ppermute | solution.py:96
  43.9 38.1 %collective-permute-start.4 = (f32[384]{0:T(512)S(1)}, f32[384]{0:T(512)S(1)}, u32[]{:S(2)}, u32[]{:S(2)}) collective-permute-start(f32[384]{0:T(512)S(1)} %select_maximum_fusion), channel_id=1, source_target_pairs={{0,5},{1,4},{2,7},{3,6},{4,1},{5,0},{6,3},{7,2},{8,13},{9,12},{10,... | collective-permute-start | bytes 4616 | tf_op jit(solution)/shard_map/ppermute | solution.py:96
  89.5 35.5 %collective-permute-start.9 = (bf16[64,5120]{1,0:T(8,128)(2,1)}, bf16[64,5120]{1,0:T(8,128)(2,1)S(1)}, u32[]{:S(2)}, u32[]{:S(2)}) collective-permute-start(bf16[64,5120]{1,0:T(8,128)(2,1)} %collective-permute-done.8), channel_id=1, source_target_pairs={{0,8},{8,0},{16,24},{24,16},{1,9},{9,1},{17,25},{25,17},{2,10},{10... | collective-permute-start | bytes 1966088 | tf_op jit(solution)/shard_map/ppermute | solution.py:159
  91.1 35.9 %collective-permute-start.10 = (bf16[64,5120]{1,0:T(8,128)(2,1)}, bf16[64,5120]{1,0:T(8,128)(2,1)S(1)}, u32[]{:S(2)}, u32[]{:S(2)}) collective-permute-start(bf16[64,5120]{1,0:T(8,128)(2,1)} %collective-permute-done.8), channel_id=1, source_target_pairs={{0,16},{8,24},{16,0},{24,8},{1,17},{9,25},{17,1},{25,9},{2,18},{10... | collective-permute-start | bytes 1966088 | tf_op jit(solution)/shard_map/ppermute | solution.py:160
  92.6 37.1 %collective-permute-start.15 = (bf16[64,5120]{1,0:T(8,128)(2,1)S(1)}, bf16[64,5120]{1,0:T(8,128)(2,1)S(1)}, u32[]{:S(2)}, u32[]{:S(2)}) collective-permute-start(bf16[64,5120]{1,0:T(8,128)(2,1)S(1)} %collective-permute-done.14), channel_id=1, source_target_pairs={{0,8},{8,0},{16,24},{24,16},{1,9},{9,1},{17,25},{25,17},{2,10},{10... | collective-permute-start | bytes 1966088 | tf_op jit(solution)/shard_map/ppermute | solution.py:159
  95.5 36.7 %collective-permute-start.16 = (bf16[64,5120]{1,0:T(8,128)(2,1)S(1)}, bf16[64,5120]{1,0:T(8,128)(2,1)S(1)}, u32[]{:S(2)}, u32[]{:S(2)}) collective-permute-start(bf16[64,5120]{1,0:T(8,128)(2,1)S(1)} %collective-permute-done.14), channel_id=1, source_target_pairs={{0,16},{8,24},{16,0},{24,8},{1,17},{9,25},{17,1},{25,9},{2,18},{10... | collective-permute-start | bytes 1966088 | tf_op jit(solution)/shard_map/ppermute | solution.py:160
  125.1 29.4 %collective-permute-start.41 = (bf16[64,5120]{1,0:T(8,128)(2,1)S(1)}, bf16[64,5120]{1,0:T(8,128)(2,1)S(1)}, u32[]{:S(2)}, u32[]{:S(2)}) collective-permute-start(bf16[64,5120]{1,0:T(8,128)(2,1)S(1)} %collective-permute-done.14), channel_id=1, source_target_pairs={{2,4},{3,5},{4,2},{5,3},{10,12},{11,13},{12,10},{13,11},{18,20},{1... | collective-permute-start | bytes 1966088 | tf_op jit(solution)/shard_map/ppermute | solution.py:170
  127.0 43.2 %collective-permute-start.22 = (bf16[64,5120]{1,0:T(8,128)(2,1)S(1)}, bf16[64,5120]{1,0:T(8,128)(2,1)S(1)}, u32[]{:S(2)}, u32[]{:S(2)}) collective-permute-start(bf16[64,5120]{1,0:T(8,128)(2,1)S(1)} %get-tuple-element.110), channel_id=1, source_target_pairs={{0,8},{8,0},{16,24},{24,16},{1,9},{9,1},{17,25},{25,17},{2,10},{10... | collective-permute-start | bytes 1966088 | tf_op jit(solution)/shard_map/ppermute | solution.py:159
  129.8 54.3 %collective-permute-start.23 = (bf16[64,5120]{1,0:T(8,128)(2,1)S(1)}, bf16[64,5120]{1,0:T(8,128)(2,1)S(1)}, u32[]{:S(2)}, u32[]{:S(2)}) collective-permute-start(bf16[64,5120]{1,0:T(8,128)(2,1)S(1)} %get-tuple-element.110), channel_id=1, source_target_pairs={{0,16},{8,24},{16,0},{24,8},{1,17},{9,25},{17,1},{25,9},{2,18},{10... | collective-permute-start | bytes 1966088 | tf_op jit(solution)/shard_map/ppermute | solution.py:160
  153.0 31.6 %collective-permute-start.29 = (bf16[64,5120]{1,0:T(8,128)(2,1)S(1)}, bf16[64,5120]{1,0:T(8,128)(2,1)S(1)}, u32[]{:S(2)}, u32[]{:S(2)}) collective-permute-start(bf16[64,5120]{1,0:T(8,128)(2,1)S(1)} %get-tuple-element.108), channel_id=1, source_target_pairs={{0,8},{8,0},{16,24},{24,16},{1,9},{9,1},{17,25},{25,17},{2,10},{10... | collective-permute-start | bytes 1966088 | tf_op jit(solution)/shard_map/ppermute | solution.py:159
  154.5 31.5 %collective-permute-start.30 = (bf16[64,5120]{1,0:T(8,128)(2,1)S(1)}, bf16[64,5120]{1,0:T(8,128)(2,1)S(1)}, u32[]{:S(2)}, u32[]{:S(2)}) collective-permute-start(bf16[64,5120]{1,0:T(8,128)(2,1)S(1)} %get-tuple-element.108), channel_id=1, source_target_pairs={{0,16},{8,24},{16,0},{24,8},{1,17},{9,25},{17,1},{25,9},{2,18},{10... | collective-permute-start | bytes 1966088 | tf_op jit(solution)/shard_map/ppermute | solution.py:160
  170.2 51.3 %collective-permute-start.36 = (bf16[64,5120]{1,0:T(8,128)(2,1)S(1)}, bf16[64,5120]{1,0:T(8,128)(2,1)S(1)}, u32[]{:S(2)}, u32[]{:S(2)}) collective-permute-start(bf16[64,5120]{1,0:T(8,128)(2,1)S(1)} %get-tuple-element.114), channel_id=1, source_target_pairs={{0,8},{8,0},{16,24},{24,16},{1,9},{9,1},{17,25},{25,17},{2,10},{10... | collective-permute-start | bytes 1966088 | tf_op jit(solution)/shard_map/ppermute | solution.py:159
  181.5 41.5 %collective-permute-start.37 = (bf16[64,5120]{1,0:T(8,128)(2,1)S(1)}, bf16[64,5120]{1,0:T(8,128)(2,1)S(1)}, u32[]{:S(2)}, u32[]{:S(2)}) collective-permute-start(bf16[64,5120]{1,0:T(8,128)(2,1)S(1)} %get-tuple-element.114), channel_id=1, source_target_pairs={{0,16},{8,24},{16,0},{24,8},{1,17},{9,25},{17,1},{25,9},{2,18},{10... | collective-permute-start | bytes 1966088 | tf_op jit(solution)/shard_map/ppermute | solution.py:160
  184.1 41.2 %collective-permute-start.43 = (bf16[64,5120]{1,0:T(8,128)(2,1)S(1)}, bf16[64,5120]{1,0:T(8,128)(2,1)S(1)}, u32[]{:S(2)}, u32[]{:S(2)}) collective-permute-start(bf16[64,5120]{1,0:T(8,128)(2,1)S(1)} %get-tuple-element.112), channel_id=1, source_target_pairs={{0,8},{8,0},{16,24},{24,16},{1,9},{9,1},{17,25},{25,17},{2,10},{10... | collective-permute-start | bytes 1966088 | tf_op jit(solution)/shard_map/ppermute | solution.py:159
  184.6 41.9 %collective-permute-start.44 = (bf16[64,5120]{1,0:T(8,128)(2,1)S(1)}, bf16[64,5120]{1,0:T(8,128)(2,1)S(1)}, u32[]{:S(2)}, u32[]{:S(2)}) collective-permute-start(bf16[64,5120]{1,0:T(8,128)(2,1)S(1)} %get-tuple-element.112), channel_id=1, source_target_pairs={{0,16},{8,24},{16,0},{24,8},{1,17},{9,25},{17,1},{25,9},{2,18},{10... | collective-permute-start | bytes 1966088 | tf_op jit(solution)/shard_map/ppermute | solution.py:160
  220.6 30.2 %collective-permute-start.13 = (bf16[256,5120]{1,0:T(8,128)(2,1)}, bf16[256,5120]{1,0:T(8,128)(2,1)}, u32[]{:S(2)}, u32[]{:S(2)}) collective-permute-start(bf16[256,5120]{1,0:T(8,128)(2,1)} %get-tuple-element.159), channel_id=1, source_target_pairs={{0,1},{1,0},{2,3},{3,2},{4,5},{5,4},{6,7},{7,6},{8,9},{9,8},{10,11... | collective-permute-start | bytes 7864328 | tf_op jit(solution)/shard_map/ppermute | solution.py:179
  221.4 79.0 %collective-permute-start.7 = (bf16[512,5120]{1,0:T(8,128)(2,1)}, bf16[512,5120]{1,0:T(8,128)(2,1)}, u32[]{:S(2)}, u32[]{:S(2)}) collective-permute-start(bf16[512,5120]{1,0:T(8,128)(2,1)} %fusion.2), channel_id=1, source_target_pairs={{0,1},{1,0},{2,3},{3,2},{4,5},{5,4},{6,7},{7,6},{8,9},{9,8},{10,11... | collective-permute-start | bytes 15728648 | tf_op jit(solution)/shard_map/ppermute | solution.py:155
  223.0 34.3 %collective-permute-start.17 = (bf16[32,5120]{1,0:T(8,128)(2,1)}, bf16[32,5120]{1,0:T(8,128)(2,1)}, u32[]{:S(2)}, u32[]{:S(2)}) collective-permute-start(bf16[32,5120]{1,0:T(8,128)(2,1)} %slice.184), channel_id=1, source_target_pairs={{0,16},{8,24},{16,0},{24,8},{1,17},{9,25},{17,1},{25,9},{2,18},{10... | collective-permute-start | bytes 983048 | tf_op jit(solution)/shard_map/ppermute | solution.py:161
  225.3 34.4 %collective-permute-start.18 = (bf16[32,5120]{1,0:T(8,128)(2,1)S(1)}, bf16[32,5120]{1,0:T(8,128)(2,1)}, u32[]{:S(2)}, u32[]{:S(2)}) collective-permute-start(bf16[32,5120]{1,0:T(8,128)(2,1)S(1)} %slice.185), channel_id=1, source_target_pairs={{0,8},{8,0},{16,24},{24,16},{1,9},{9,1},{17,25},{25,17},{2,10},{10... | collective-permute-start | bytes 983048 | tf_op jit(solution)/shard_map/ppermute | solution.py:162
  367.5 44.7 %all-to-all-start.1 = ((bf16[8,160,640]{2,1,0:T(8,128)(2,1)}), bf16[8,160,640]{2,1,0:T(8,128)(2,1)}, u32[]{:S(2)}, u32[]{:S(2)}) async-start(bf16[8,160,640]{2,1,0:T(8,128)(2,1)} %bitcast.46), calls=%async_computation.1 | async-start | bytes 3276800 | tf_op jit(solution)/shard_map/all_to_all | solution.py:273
  (73 other events, 979.8 us)
